TPU v7x, 32 devices: a whole 2x2x4 slice. The times are simulated.
32 devices in a mesh: lev: 2 (over x), gx: 8 (over z, y), gy: 2 (over core).
Axes of the slice: x: 2, y: 2, z: 4, core: 2. Of those that a mesh axis runs over, the one named last changes fastest.
Arguments:
- increments: float32 [1, 2, 80, 128, 256], P(None, None, 'lev', 'gx', 'gy'), may hold values from -6 to 6
- vert_corr: float32 [2, 80, 80], replicated, may hold values from -0.025 to 1, as said below
- kappa: float32 [2, 128, 256], P(None, 'gx', 'gy'), may hold values from 0.03 to 0.24
- sea_mask: int32 [80, 128, 256], P('lev', 'gx', 'gy'), may hold values 0 or 1
- level_count: int32 [128, 256], P('gx', 'gy'), may hold values from 10 to 75
Outputs:
- covaried: float32 [1, 2, 80, 128, 256], P(None, None, 'lev', 'gx', 'gy')
Inputs may be any that keep to these rules, and one draw needn't show every extreme that they name: vert_corr has ones on the diagonal, and each row's other entries together have magnitude below one.
All inputs are finite; a program needn't handle non-finite values. No bound on the sum of `sea_mask` on one device may be relied on, other than what follows from the above.
Results may differ from a plain program's by a relative error of at most 0.00021.
Values sent between devices are 32-bit elements; how exact they have to be, the bound alone decides.
A program may use at most 64 MiB of HBM per device.

v0:
```python
import jax
import jax.numpy as jnp
from jax import lax
from jax.sharding import PartitionSpec as P

PASSES = 10


def from_behind(block, axis, distance):
    devices = range(lax.axis_size(axis))
    route = [((i - distance) % len(devices), i) for i in devices]
    return lax.ppermute(block, axis, route)


def shifted(block, axis, distance):
    devices = range(lax.axis_size(axis))
    route = [(i - distance, i) for i in devices if i - distance in devices]
    return lax.ppermute(block, axis, route)


def padded(cells, sides, width):
    for axis, dim in sides:
        count = lax.axis_size(axis)
        head = lax.slice_in_dim(cells, 0, width, axis=dim)
        tail = lax.slice_in_dim(cells, cells.shape[dim] - width, cells.shape[dim], axis=dim)
        cells = jnp.concatenate(
            [
                lax.ppermute(tail, axis, [(i, (i + 1) % count) for i in range(count)]),
                cells,
                lax.ppermute(head, axis, [((i + 1) % count, i) for i in range(count)]),
            ],
            axis=dim,
        )
    return cells


def relax(extended, east_ext, north_ext, wet_center):
    center = extended[..., 1:-1, 1:-1]
    flux = east_ext[1:-1, 1:-1] * (extended[..., 2:, 1:-1] - center)
    flux = flux + east_ext[:-2, 1:-1] * (extended[..., :-2, 1:-1] - center)
    flux = flux + north_ext[1:-1, 1:-1] * (extended[..., 1:-1, 2:] - center)
    flux = flux + north_ext[1:-1, :-2] * (extended[..., 1:-1, :-2] - center)
    return wet_center * (center + flux)


def per_device(increments, vert_corr, kappa, sea_mask, level_count):
    lev_dev = sea_mask.shape[0]
    cells_x = sea_mask.shape[1]
    cells_y = sea_mask.shape[2]
    lev_first = lax.axis_index("lev") * lev_dev
    levels = lev_first + jnp.arange(lev_dev, dtype=jnp.int32)
    wet = sea_mask * (levels[:, None, None] < level_count[None]).astype(jnp.int32)
    wet_float = wet.astype(jnp.float32)
    masked = increments * wet_float
    own_rows = lax.dynamic_slice_in_dim(vert_corr, lev_first, lev_dev, 1)
    correlated = jnp.einsum(
        "toh,dthxy->dtoxy",
        own_rows,
        lax.all_gather(masked, "lev", axis=2, tiled=True),
        precision=lax.Precision.HIGHEST,
    )
    field = correlated * wet_float
    total_y = cells_y * lax.axis_size("gy")
    local_rows = lax.axis_index("gy") * cells_y + jnp.arange(cells_y, dtype=jnp.int32)
    open_local = (local_rows != total_y - 1).astype(jnp.float32)
    east_local = kappa[0]
    north_local = kappa[1] * open_local[None, :]
    east_low = from_behind(east_local[-1:, :], "gx", 1)
    north_low = shifted(north_local[:, -1:], "gy", 1)
    zero_row = jnp.zeros((1, cells_y), jnp.float32)
    zero_col = jnp.zeros((cells_x, 1), jnp.float32)
    east_ext = jnp.pad(jnp.concatenate([east_low, east_local, zero_row], axis=0), ((0, 0), (1, 1)))
    north_ext = jnp.pad(
        jnp.concatenate([north_low, north_local, zero_col], axis=1), ((1, 1), (0, 0))
    )

    def one_pass(step, current):
        extended = padded(current, (("gx", 3), ("gy", 4)), 1)
        return relax(extended, east_ext, north_ext, wet_float)

    field = lax.fori_loop(0, PASSES, one_pass, field)
    return field


def solution(mesh):
    in_specs = (
        P(None, None, "lev", "gx", "gy"),
        P(),
        P(None, "gx", "gy"),
        P("lev", "gx", "gy"),
        P("gx", "gy"),
    )
    out_specs = P(None, None, "lev", "gx", "gy")
    return jax.shard_map(
        per_device, mesh=mesh, in_specs=in_specs, out_specs=out_specs, check_vma=False
    )
```

profile of v0, /device:TPU:0, one launch (start us, length us, event | category | flops | bytes accessed | tf_op | source)
XLA Modules:
  0.0 171.8 jit_solution(11940098655885477659)
XLA Ops:
  7.7 2.1 %copy_multiply_fusion = f32[1,2,40,16,128]{4,2,3,1,0:T(8,128)} fusion(f32[1,2,40,16,128]{4,3,2,1,0:T(8,128)} %param.7, f32[40,16,128]{2,0,1:T(8,128)S(1)} %fusion.21), kind=kLoop, calls=%fused_computation.24 | loop fusion | flops 163840 | bytes 1638400 | tf_op jit(solution)/shard_map/mul | solution.py:54
  9.9 3.0 %collective-permute-start.4 = (f32[1,128]{1,0:T(1,128)S(1)}, f32[1,128]{1,0:T(1,128)S(1)}, u32[]{:S(2)}, u32[]{:S(2)}) collective-permute-start(f32[1,128]{1,0:T(1,128)S(1)} %slice_bitcast_fusion.1), channel_id=1, source_target_pairs={{14,0},{0,2},{2,4},{4,6},{6,8},{8,10},{10,12},{12,14},{15,1},{1,3}... | collective-permute-start | bytes 1544 | tf_op jit(solution)/shard_map/ppermute | solution.py:12
  15.3 2.1 %collective-permute-done.4 = f32[1,128]{1,0:T(1,128)S(1)} collective-permute-done((f32[1,128]{1,0:T(1,128)S(1)}, f32[1,128]{1,0:T(1,128)S(1)}, u32[]{:S(2)}, u32[]{:S(2)}) %collective-permute-start.4) | collective-permute-done | bytes 544 | tf_op jit(solution)/shard_map/ppermute | solution.py:12
  17.6 19.4 %all-gather.2.cloned.1.call-done = f32[1,2,80,16,128]{4,2,3,1,0:T(8,128)} async-done(((f32[1,2,40,16,128]{4,2,3,1,0:T(8,128)}), f32[1,2,80,16,128]{4,2,3,1,0:T(8,128)}) %all-gather.2.cloned.1.call-update) | async-done | bytes 1310736 | tf_op jit(solution)/shard_map/all_gather | solution.py:59
  37.0 3.0 %fusion.18 = f32[1,2,40,16,128]{4,2,3,1,0:T(8,128)} fusion(f32[1,2,80,16,128]{4,2,3,1,0:T(8,128)} %all-gather.2.cloned.1.call-done, f32[40,16,128]{2,0,1:T(8,128)S(1)} %fusion.21, f32[2,80,80]{2,1,0:T(8,128)S(1)} %copy-done, s32[]{:T(128)S(6)} %select_n.3), kind=kOutput, calls=%fused_computation.23 | convolution fusion | flops 157450240 | bytes 2334724 | tf_op jit(solution)/shard_map/toh,dthxy->dtoxy/dot_general | solution.py:56
  40.0 122.9 %while.10 = (s32[]{:T(128)}, f32[1,2,40,16,128]{4,2,3,1,0:T(8,128)}, f32[40,16,128]{2,0,1:T(8,128)S(1)}, f32[18,130]{1,0:T(8,128)S(1)}, f32[18,130]{1,0:T(8,128)S(1)}, /*index=5*/s32[]{:T(128)}) while((s32[]{:T(128)}, f32[1,2,40,16,128]{4,2,3,1,0:T(8,128)}, f32[40,16,128]{2,0,1:T(8,128)S(1)}, f32[18,130]{1,0:T(8,128)S(1)}, ...), condition=%wide.region_1.2_spmd, body=%wide.region_0.1_spmd.sunk | while | flops 2785282 | bytes 5959653 | solution.py:81
  41.1 1.5 collective-permute-start
  42.6 3.2 %collective-permute-start.1 = (f32[1,2,40,1,128]{4,2,3,1,0:T(8,128)S(1)}, f32[1,2,40,1,128]{4,2,3,1,0:T(8,128)S(1)}, u32[]{:S(2)}, u32[]{:S(2)}) collective-permute-start(f32[1,2,40,1,128]{4,2,3,1,0:T(8,128)S(1)} %get-tuple-element.103), channel_id=1, source_target_pairs={{2,0},{4,2},{6,4},{8,6},{10,8},{12,10},{14,12},{0,14},{3,1},{5,3},... | collective-permute-start | bytes 122888 | tf_op jit(solution)/shard_map/while/body/eval_jaxpr/ppermute | solution.py:30
  45.8 2.0 %collective-permute-done = f32[1,2,40,1,128]{4,2,3,1,0:T(8,128)S(1)} collective-permute-done((f32[1,2,40,1,128]{4,2,3,1,0:T(8,128)S(1)}, f32[1,2,40,1,128]{4,2,3,1,0:T(8,128)S(1)}, u32[]{:S(2)}, u32[]{:S(2)}) %collective-permute-start) | collective-permute-done | bytes 40992 | tf_op jit(solution)/shard_map/while/body/eval_jaxpr/ppermute | solution.py:28
  50.8 1.5 fusion.36
  54.5 3.6 %collective-permute-start.1 = (f32[1,2,40,1,128]{4,2,3,1,0:T(8,128)S(1)}, f32[1,2,40,1,128]{4,2,3,1,0:T(8,128)S(1)}, u32[]{:S(2)}, u32[]{:S(2)}) collective-permute-start(f32[1,2,40,1,128]{4,2,3,1,0:T(8,128)S(1)} %get-tuple-element.103), channel_id=1, source_target_pairs={{2,0},{4,2},{6,4},{8,6},{10,8},{12,10},{14,12},{0,14},{3,1},{5,3},... | collective-permute-start | bytes 122888 | tf_op jit(solution)/shard_map/while/body/eval_jaxpr/ppermute | solution.py:30
  58.1 2.0 %collective-permute-done = f32[1,2,40,1,128]{4,2,3,1,0:T(8,128)S(1)} collective-permute-done((f32[1,2,40,1,128]{4,2,3,1,0:T(8,128)S(1)}, f32[1,2,40,1,128]{4,2,3,1,0:T(8,128)S(1)}, u32[]{:S(2)}, u32[]{:S(2)}) %collective-permute-start) | collective-permute-done | bytes 40992 | tf_op jit(solution)/shard_map/while/body/eval_jaxpr/ppermute | solution.py:28
  65.7 4.7 %collective-permute-start.1 = (f32[1,2,40,1,128]{4,2,3,1,0:T(8,128)S(1)}, f32[1,2,40,1,128]{4,2,3,1,0:T(8,128)S(1)}, u32[]{:S(2)}, u32[]{:S(2)}) collective-permute-start(f32[1,2,40,1,128]{4,2,3,1,0:T(8,128)S(1)} %get-tuple-element.103), channel_id=1, source_target_pairs={{2,0},{4,2},{6,4},{8,6},{10,8},{12,10},{14,12},{0,14},{3,1},{5,3},... | collective-permute-start | bytes 122888 | tf_op jit(solution)/shard_map/while/body/eval_jaxpr/ppermute | solution.py:30
  70.4 2.0 %collective-permute-done = f32[1,2,40,1,128]{4,2,3,1,0:T(8,128)S(1)} collective-permute-done((f32[1,2,40,1,128]{4,2,3,1,0:T(8,128)S(1)}, f32[1,2,40,1,128]{4,2,3,1,0:T(8,128)S(1)}, u32[]{:S(2)}, u32[]{:S(2)}) %collective-permute-start) | collective-permute-done | bytes 40992 | tf_op jit(solution)/shard_map/while/body/eval_jaxpr/ppermute | solution.py:28
  77.9 4.7 %collective-permute-start.1 = (f32[1,2,40,1,128]{4,2,3,1,0:T(8,128)S(1)}, f32[1,2,40,1,128]{4,2,3,1,0:T(8,128)S(1)}, u32[]{:S(2)}, u32[]{:S(2)}) collective-permute-start(f32[1,2,40,1,128]{4,2,3,1,0:T(8,128)S(1)} %get-tuple-element.103), channel_id=1, source_target_pairs={{2,0},{4,2},{6,4},{8,6},{10,8},{12,10},{14,12},{0,14},{3,1},{5,3},... | collective-permute-start | bytes 122888 | tf_op jit(solution)/shard_map/while/body/eval_jaxpr/ppermute | solution.py:30
  82.6 2.0 %collective-permute-done = f32[1,2,40,1,128]{4,2,3,1,0:T(8,128)S(1)} collective-permute-done((f32[1,2,40,1,128]{4,2,3,1,0:T(8,128)S(1)}, f32[1,2,40,1,128]{4,2,3,1,0:T(8,128)S(1)}, u32[]{:S(2)}, u32[]{:S(2)}) %collective-permute-start) | collective-permute-done | bytes 40992 | tf_op jit(solution)/shard_map/while/body/eval_jaxpr/ppermute | solution.py:28
  87.7 1.5 fusion.36
  90.2 4.7 %collective-permute-start.1 = (f32[1,2,40,1,128]{4,2,3,1,0:T(8,128)S(1)}, f32[1,2,40,1,128]{4,2,3,1,0:T(8,128)S(1)}, u32[]{:S(2)}, u32[]{:S(2)}) collective-permute-start(f32[1,2,40,1,128]{4,2,3,1,0:T(8,128)S(1)} %get-tuple-element.103), channel_id=1, source_target_pairs={{2,0},{4,2},{6,4},{8,6},{10,8},{12,10},{14,12},{0,14},{3,1},{5,3},... | collective-permute-start | bytes 122888 | tf_op jit(solution)/shard_map/while/body/eval_jaxpr/ppermute | solution.py:30
  95.0 2.0 %collective-permute-done = f32[1,2,40,1,128]{4,2,3,1,0:T(8,128)S(1)} collective-permute-done((f32[1,2,40,1,128]{4,2,3,1,0:T(8,128)S(1)}, f32[1,2,40,1,128]{4,2,3,1,0:T(8,128)S(1)}, u32[]{:S(2)}, u32[]{:S(2)}) %collective-permute-start) | collective-permute-done | bytes 40992 | tf_op jit(solution)/shard_map/while/body/eval_jaxpr/ppermute | solution.py:28
  100.0 1.5 fusion.36
  102.5 4.7 %collective-permute-start.1 = (f32[1,2,40,1,128]{4,2,3,1,0:T(8,128)S(1)}, f32[1,2,40,1,128]{4,2,3,1,0:T(8,128)S(1)}, u32[]{:S(2)}, u32[]{:S(2)}) collective-permute-start(f32[1,2,40,1,128]{4,2,3,1,0:T(8,128)S(1)} %get-tuple-element.103), channel_id=1, source_target_pairs={{2,0},{4,2},{6,4},{8,6},{10,8},{12,10},{14,12},{0,14},{3,1},{5,3},... | collective-permute-start | bytes 122888 | tf_op jit(solution)/shard_map/while/body/eval_jaxpr/ppermute | solution.py:30
  107.2 2.0 %collective-permute-done = f32[1,2,40,1,128]{4,2,3,1,0:T(8,128)S(1)} collective-permute-done((f32[1,2,40,1,128]{4,2,3,1,0:T(8,128)S(1)}, f32[1,2,40,1,128]{4,2,3,1,0:T(8,128)S(1)}, u32[]{:S(2)}, u32[]{:S(2)}) %collective-permute-start) | collective-permute-done | bytes 40992 | tf_op jit(solution)/shard_map/while/body/eval_jaxpr/ppermute | solution.py:28
  114.8 4.7 %collective-permute-start.1 = (f32[1,2,40,1,128]{4,2,3,1,0:T(8,128)S(1)}, f32[1,2,40,1,128]{4,2,3,1,0:T(8,128)S(1)}, u32[]{:S(2)}, u32[]{:S(2)}) collective-permute-start(f32[1,2,40,1,128]{4,2,3,1,0:T(8,128)S(1)} %get-tuple-element.103), channel_id=1, source_target_pairs={{2,0},{4,2},{6,4},{8,6},{10,8},{12,10},{14,12},{0,14},{3,1},{5,3},... | collective-permute-start | bytes 122888 | tf_op jit(solution)/shard_map/while/body/eval_jaxpr/ppermute | solution.py:30
  119.5 2.0 %collective-permute-done = f32[1,2,40,1,128]{4,2,3,1,0:T(8,128)S(1)} collective-permute-done((f32[1,2,40,1,128]{4,2,3,1,0:T(8,128)S(1)}, f32[1,2,40,1,128]{4,2,3,1,0:T(8,128)S(1)}, u32[]{:S(2)}, u32[]{:S(2)}) %collective-permute-start) | collective-permute-done | bytes 40992 | tf_op jit(solution)/shard_map/while/body/eval_jaxpr/ppermute | solution.py:28
  127.1 4.7 %collective-permute-start.1 = (f32[1,2,40,1,128]{4,2,3,1,0:T(8,128)S(1)}, f32[1,2,40,1,128]{4,2,3,1,0:T(8,128)S(1)}, u32[]{:S(2)}, u32[]{:S(2)}) collective-permute-start(f32[1,2,40,1,128]{4,2,3,1,0:T(8,128)S(1)} %get-tuple-element.103), channel_id=1, source_target_pairs={{2,0},{4,2},{6,4},{8,6},{10,8},{12,10},{14,12},{0,14},{3,1},{5,3},... | collective-permute-start | bytes 122888 | tf_op jit(solution)/shard_map/while/body/eval_jaxpr/ppermute | solution.py:30
  131.8 2.0 %collective-permute-done = f32[1,2,40,1,128]{4,2,3,1,0:T(8,128)S(1)} collective-permute-done((f32[1,2,40,1,128]{4,2,3,1,0:T(8,128)S(1)}, f32[1,2,40,1,128]{4,2,3,1,0:T(8,128)S(1)}, u32[]{:S(2)}, u32[]{:S(2)}) %collective-permute-start) | collective-permute-done | bytes 40992 | tf_op jit(solution)/shard_map/while/body/eval_jaxpr/ppermute | solution.py:28
  136.9 1.5 fusion.36
  139.4 4.7 %collective-permute-start.1 = (f32[1,2,40,1,128]{4,2,3,1,0:T(8,128)S(1)}, f32[1,2,40,1,128]{4,2,3,1,0:T(8,128)S(1)}, u32[]{:S(2)}, u32[]{:S(2)}) collective-permute-start(f32[1,2,40,1,128]{4,2,3,1,0:T(8,128)S(1)} %get-tuple-element.103), channel_id=1, source_target_pairs={{2,0},{4,2},{6,4},{8,6},{10,8},{12,10},{14,12},{0,14},{3,1},{5,3},... | collective-permute-start | bytes 122888 | tf_op jit(solution)/shard_map/while/body/eval_jaxpr/ppermute | solution.py:30
  144.1 2.0 %collective-permute-done = f32[1,2,40,1,128]{4,2,3,1,0:T(8,128)S(1)} collective-permute-done((f32[1,2,40,1,128]{4,2,3,1,0:T(8,128)S(1)}, f32[1,2,40,1,128]{4,2,3,1,0:T(8,128)S(1)}, u32[]{:S(2)}, u32[]{:S(2)}) %collective-permute-start) | collective-permute-done | bytes 40992 | tf_op jit(solution)/shard_map/while/body/eval_jaxpr/ppermute | solution.py:28
  151.7 4.7 %collective-permute-start.1 = (f32[1,2,40,1,128]{4,2,3,1,0:T(8,128)S(1)}, f32[1,2,40,1,128]{4,2,3,1,0:T(8,128)S(1)}, u32[]{:S(2)}, u32[]{:S(2)}) collective-permute-start(f32[1,2,40,1,128]{4,2,3,1,0:T(8,128)S(1)} %get-tuple-element.103), channel_id=1, source_target_pairs={{2,0},{4,2},{6,4},{8,6},{10,8},{12,10},{14,12},{0,14},{3,1},{5,3},... | collective-permute-start | bytes 122888 | tf_op jit(solution)/shard_map/while/body/eval_jaxpr/ppermute | solution.py:30
  156.4 2.0 %collective-permute-done = f32[1,2,40,1,128]{4,2,3,1,0:T(8,128)S(1)} collective-permute-done((f32[1,2,40,1,128]{4,2,3,1,0:T(8,128)S(1)}, f32[1,2,40,1,128]{4,2,3,1,0:T(8,128)S(1)}, u32[]{:S(2)}, u32[]{:S(2)}) %collective-permute-start) | collective-permute-done | bytes 40992 | tf_op jit(solution)/shard_map/while/body/eval_jaxpr/ppermute | solution.py:28
  162.9 2.0 %copy.20 = f32[1,2,40,16,128]{4,3,2,1,0:T(8,128)} copy(f32[1,2,40,16,128]{4,2,3,1,0:T(8,128)} %get-tuple-element.32) | data formatting | bytes 1310720 | tf_op jit(solution)/shard_map/while | solution.py:81
  (196 shorter events, 54.5 us)
Async XLA Ops:
  6.5 30.4 %all-gather.2.cloned.1.call-start = ((), (), s32[]{:S(2)}) async-start(), calls=%async_computation | async-start | bytes 1966080 | tf_op jit(solution)/shard_map/all_gather | solution.py:59
  9.9 7.6 %collective-permute-start.4 = (f32[1,128]{1,0:T(1,128)S(1)}, f32[1,128]{1,0:T(1,128)S(1)}, u32[]{:S(2)}, u32[]{:S(2)}) collective-permute-start(f32[1,128]{1,0:T(1,128)S(1)} %slice_bitcast_fusion.1), channel_id=1, source_target_pairs={{14,0},{0,2},{2,4},{4,6},{6,8},{8,10},{10,12},{12,14},{15,1},{1,3}... | collective-permute-start | bytes 1544 | tf_op jit(solution)/shard_map/ppermute | solution.py:12
  13.0 2.3 %collective-permute-start.5 = (f32[16,1]{1,0:T(8,128)S(1)}, f32[16,1]{1,0:T(8,128)S(1)}, u32[]{:S(2)}, u32[]{:S(2)}) collective-permute-start(f32[16,1]{1,0:T(8,128)S(1)} %slice.63), channel_id=1, source_target_pairs={{0,1},{2,3},{4,5},{6,7},{8,9},{10,11},{12,13},{14,15},{16,17},{18,... | collective-permute-start | bytes 200 | tf_op jit(solution)/shard_map/ppermute | solution.py:18
  41.1 6.7 %collective-permute-start = (f32[1,2,40,1,128]{4,2,3,1,0:T(8,128)S(1)}, f32[1,2,40,1,128]{4,2,3,1,0:T(8,128)S(1)}, u32[]{:S(2)}, u32[]{:S(2)}) collective-permute-start(f32[1,2,40,1,128]{4,2,3,1,0:T(8,128)S(1)} %get-tuple-element.102), channel_id=1, source_target_pairs={{0,2},{2,4},{4,6},{6,8},{8,10},{10,12},{12,14},{14,0},{1,3},{3,5},... | collective-permute-start | bytes 122888 | tf_op jit(solution)/shard_map/while/body/eval_jaxpr/ppermute | solution.py:28
  42.6 5.2 %collective-permute-start.1 = (f32[1,2,40,1,128]{4,2,3,1,0:T(8,128)S(1)}, f32[1,2,40,1,128]{4,2,3,1,0:T(8,128)S(1)}, u32[]{:S(2)}, u32[]{:S(2)}) collective-permute-start(f32[1,2,40,1,128]{4,2,3,1,0:T(8,128)S(1)} %get-tuple-element.103), channel_id=1, source_target_pairs={{2,0},{4,2},{6,4},{8,6},{10,8},{12,10},{14,12},{0,14},{3,1},{5,3},... | collective-permute-start | bytes 122888 | tf_op jit(solution)/shard_map/while/body/eval_jaxpr/ppermute | solution.py:30
  48.7 1.8 %collective-permute-start.3 = (f32[1,2,40,18,1]{2,1,4,3,0:T(2,128)S(1)}, f32[1,2,40,18,1]{2,1,4,3,0:T(2,128)S(1)}, u32[]{:S(2)}, u32[]{:S(2)}) collective-permute-start(f32[1,2,40,18,1]{2,1,4,3,0:T(2,128)S(1)} %copy.34), channel_id=1, source_target_pairs={{1,0},{0,1},{3,2},{2,3},{5,4},{4,5},{7,6},{6,7},{9,8},{8,9},{11,10... | collective-permute-start | bytes 17288 | tf_op jit(solution)/shard_map/while/body/eval_jaxpr/ppermute | solution.py:30
  53.3 6.7 %collective-permute-start = (f32[1,2,40,1,128]{4,2,3,1,0:T(8,128)S(1)}, f32[1,2,40,1,128]{4,2,3,1,0:T(8,128)S(1)}, u32[]{:S(2)}, u32[]{:S(2)}) collective-permute-start(f32[1,2,40,1,128]{4,2,3,1,0:T(8,128)S(1)} %get-tuple-element.102), channel_id=1, source_target_pairs={{0,2},{2,4},{4,6},{6,8},{8,10},{10,12},{12,14},{14,0},{1,3},{3,5},... | collective-permute-start | bytes 122888 | tf_op jit(solution)/shard_map/while/body/eval_jaxpr/ppermute | solution.py:28
  54.5 5.7 %collective-permute-start.1 = (f32[1,2,40,1,128]{4,2,3,1,0:T(8,128)S(1)}, f32[1,2,40,1,128]{4,2,3,1,0:T(8,128)S(1)}, u32[]{:S(2)}, u32[]{:S(2)}) collective-permute-start(f32[1,2,40,1,128]{4,2,3,1,0:T(8,128)S(1)} %get-tuple-element.103), channel_id=1, source_target_pairs={{2,0},{4,2},{6,4},{8,6},{10,8},{12,10},{14,12},{0,14},{3,1},{5,3},... | collective-permute-start | bytes 122888 | tf_op jit(solution)/shard_map/while/body/eval_jaxpr/ppermute | solution.py:30
  61.0 1.8 %collective-permute-start.3 = (f32[1,2,40,18,1]{2,1,4,3,0:T(2,128)S(1)}, f32[1,2,40,18,1]{2,1,4,3,0:T(2,128)S(1)}, u32[]{:S(2)}, u32[]{:S(2)}) collective-permute-start(f32[1,2,40,18,1]{2,1,4,3,0:T(2,128)S(1)} %copy.34), channel_id=1, source_target_pairs={{1,0},{0,1},{3,2},{2,3},{5,4},{4,5},{7,6},{6,7},{9,8},{8,9},{11,10... | collective-permute-start | bytes 17288 | tf_op jit(solution)/shard_map/while/body/eval_jaxpr/ppermute | solution.py:30
  65.6 6.7 %collective-permute-start = (f32[1,2,40,1,128]{4,2,3,1,0:T(8,128)S(1)}, f32[1,2,40,1,128]{4,2,3,1,0:T(8,128)S(1)}, u32[]{:S(2)}, u32[]{:S(2)}) collective-permute-start(f32[1,2,40,1,128]{4,2,3,1,0:T(8,128)S(1)} %get-tuple-element.102), channel_id=1, source_target_pairs={{0,2},{2,4},{4,6},{6,8},{8,10},{10,12},{12,14},{14,0},{1,3},{3,5},... | collective-permute-start | bytes 122888 | tf_op jit(solution)/shard_map/while/body/eval_jaxpr/ppermute | solution.py:28
  65.7 6.7 %collective-permute-start.1 = (f32[1,2,40,1,128]{4,2,3,1,0:T(8,128)S(1)}, f32[1,2,40,1,128]{4,2,3,1,0:T(8,128)S(1)}, u32[]{:S(2)}, u32[]{:S(2)}) collective-permute-start(f32[1,2,40,1,128]{4,2,3,1,0:T(8,128)S(1)} %get-tuple-element.103), channel_id=1, source_target_pairs={{2,0},{4,2},{6,4},{8,6},{10,8},{12,10},{14,12},{0,14},{3,1},{5,3},... | collective-permute-start | bytes 122888 | tf_op jit(solution)/shard_map/while/body/eval_jaxpr/ppermute | solution.py:30
  73.3 1.8 %collective-permute-start.3 = (f32[1,2,40,18,1]{2,1,4,3,0:T(2,128)S(1)}, f32[1,2,40,18,1]{2,1,4,3,0:T(2,128)S(1)}, u32[]{:S(2)}, u32[]{:S(2)}) collective-permute-start(f32[1,2,40,18,1]{2,1,4,3,0:T(2,128)S(1)} %copy.34), channel_id=1, source_target_pairs={{1,0},{0,1},{3,2},{2,3},{5,4},{4,5},{7,6},{6,7},{9,8},{8,9},{11,10... | collective-permute-start | bytes 17288 | tf_op jit(solution)/shard_map/while/body/eval_jaxpr/ppermute | solution.py:30
  77.9 6.7 %collective-permute-start = (f32[1,2,40,1,128]{4,2,3,1,0:T(8,128)S(1)}, f32[1,2,40,1,128]{4,2,3,1,0:T(8,128)S(1)}, u32[]{:S(2)}, u32[]{:S(2)}) collective-permute-start(f32[1,2,40,1,128]{4,2,3,1,0:T(8,128)S(1)} %get-tuple-element.102), channel_id=1, source_target_pairs={{0,2},{2,4},{4,6},{6,8},{8,10},{10,12},{12,14},{14,0},{1,3},{3,5},... | collective-permute-start | bytes 122888 | tf_op jit(solution)/shard_map/while/body/eval_jaxpr/ppermute | solution.py:28
  77.9 6.8 %collective-permute-start.1 = (f32[1,2,40,1,128]{4,2,3,1,0:T(8,128)S(1)}, f32[1,2,40,1,128]{4,2,3,1,0:T(8,128)S(1)}, u32[]{:S(2)}, u32[]{:S(2)}) collective-permute-start(f32[1,2,40,1,128]{4,2,3,1,0:T(8,128)S(1)} %get-tuple-element.103), channel_id=1, source_target_pairs={{2,0},{4,2},{6,4},{8,6},{10,8},{12,10},{14,12},{0,14},{3,1},{5,3},... | collective-permute-start | bytes 122888 | tf_op jit(solution)/shard_map/while/body/eval_jaxpr/ppermute | solution.py:30
  85.6 1.8 %collective-permute-start.3 = (f32[1,2,40,18,1]{2,1,4,3,0:T(2,128)S(1)}, f32[1,2,40,18,1]{2,1,4,3,0:T(2,128)S(1)}, u32[]{:S(2)}, u32[]{:S(2)}) collective-permute-start(f32[1,2,40,18,1]{2,1,4,3,0:T(2,128)S(1)} %copy.34), channel_id=1, source_target_pairs={{1,0},{0,1},{3,2},{2,3},{5,4},{4,5},{7,6},{6,7},{9,8},{8,9},{11,10... | collective-permute-start | bytes 17288 | tf_op jit(solution)/shard_map/while/body/eval_jaxpr/ppermute | solution.py:30
  90.2 6.7 %collective-permute-start = (f32[1,2,40,1,128]{4,2,3,1,0:T(8,128)S(1)}, f32[1,2,40,1,128]{4,2,3,1,0:T(8,128)S(1)}, u32[]{:S(2)}, u32[]{:S(2)}) collective-permute-start(f32[1,2,40,1,128]{4,2,3,1,0:T(8,128)S(1)} %get-tuple-element.102), channel_id=1, source_target_pairs={{0,2},{2,4},{4,6},{6,8},{8,10},{10,12},{12,14},{14,0},{1,3},{3,5},... | collective-permute-start | bytes 122888 | tf_op jit(solution)/shard_map/while/body/eval_jaxpr/ppermute | solution.py:28
  90.2 6.7 %collective-permute-start.1 = (f32[1,2,40,1,128]{4,2,3,1,0:T(8,128)S(1)}, f32[1,2,40,1,128]{4,2,3,1,0:T(8,128)S(1)}, u32[]{:S(2)}, u32[]{:S(2)}) collective-permute-start(f32[1,2,40,1,128]{4,2,3,1,0:T(8,128)S(1)} %get-tuple-element.103), channel_id=1, source_target_pairs={{2,0},{4,2},{6,4},{8,6},{10,8},{12,10},{14,12},{0,14},{3,1},{5,3},... | collective-permute-start | bytes 122888 | tf_op jit(solution)/shard_map/while/body/eval_jaxpr/ppermute | solution.py:30
  97.9 1.8 %collective-permute-start.3 = (f32[1,2,40,18,1]{2,1,4,3,0:T(2,128)S(1)}, f32[1,2,40,18,1]{2,1,4,3,0:T(2,128)S(1)}, u32[]{:S(2)}, u32[]{:S(2)}) collective-permute-start(f32[1,2,40,18,1]{2,1,4,3,0:T(2,128)S(1)} %copy.34), channel_id=1, source_target_pairs={{1,0},{0,1},{3,2},{2,3},{5,4},{4,5},{7,6},{6,7},{9,8},{8,9},{11,10... | collective-permute-start | bytes 17288 | tf_op jit(solution)/shard_map/while/body/eval_jaxpr/ppermute | solution.py:30
  102.5 6.7 %collective-permute-start = (f32[1,2,40,1,128]{4,2,3,1,0:T(8,128)S(1)}, f32[1,2,40,1,128]{4,2,3,1,0:T(8,128)S(1)}, u32[]{:S(2)}, u32[]{:S(2)}) collective-permute-start(f32[1,2,40,1,128]{4,2,3,1,0:T(8,128)S(1)} %get-tuple-element.102), channel_id=1, source_target_pairs={{0,2},{2,4},{4,6},{6,8},{8,10},{10,12},{12,14},{14,0},{1,3},{3,5},... | collective-permute-start | bytes 122888 | tf_op jit(solution)/shard_map/while/body/eval_jaxpr/ppermute | solution.py:28
  102.5 6.8 %collective-permute-start.1 = (f32[1,2,40,1,128]{4,2,3,1,0:T(8,128)S(1)}, f32[1,2,40,1,128]{4,2,3,1,0:T(8,128)S(1)}, u32[]{:S(2)}, u32[]{:S(2)}) collective-permute-start(f32[1,2,40,1,128]{4,2,3,1,0:T(8,128)S(1)} %get-tuple-element.103), channel_id=1, source_target_pairs={{2,0},{4,2},{6,4},{8,6},{10,8},{12,10},{14,12},{0,14},{3,1},{5,3},... | collective-permute-start | bytes 122888 | tf_op jit(solution)/shard_map/while/body/eval_jaxpr/ppermute | solution.py:30
  110.2 1.8 %collective-permute-start.3 = (f32[1,2,40,18,1]{2,1,4,3,0:T(2,128)S(1)}, f32[1,2,40,18,1]{2,1,4,3,0:T(2,128)S(1)}, u32[]{:S(2)}, u32[]{:S(2)}) collective-permute-start(f32[1,2,40,18,1]{2,1,4,3,0:T(2,128)S(1)} %copy.34), channel_id=1, source_target_pairs={{1,0},{0,1},{3,2},{2,3},{5,4},{4,5},{7,6},{6,7},{9,8},{8,9},{11,10... | collective-permute-start | bytes 17288 | tf_op jit(solution)/shard_map/while/body/eval_jaxpr/ppermute | solution.py:30
  114.8 6.7 %collective-permute-start = (f32[1,2,40,1,128]{4,2,3,1,0:T(8,128)S(1)}, f32[1,2,40,1,128]{4,2,3,1,0:T(8,128)S(1)}, u32[]{:S(2)}, u32[]{:S(2)}) collective-permute-start(f32[1,2,40,1,128]{4,2,3,1,0:T(8,128)S(1)} %get-tuple-element.102), channel_id=1, source_target_pairs={{0,2},{2,4},{4,6},{6,8},{8,10},{10,12},{12,14},{14,0},{1,3},{3,5},... | collective-permute-start | bytes 122888 | tf_op jit(solution)/shard_map/while/body/eval_jaxpr/ppermute | solution.py:28
  114.8 6.7 %collective-permute-start.1 = (f32[1,2,40,1,128]{4,2,3,1,0:T(8,128)S(1)}, f32[1,2,40,1,128]{4,2,3,1,0:T(8,128)S(1)}, u32[]{:S(2)}, u32[]{:S(2)}) collective-permute-start(f32[1,2,40,1,128]{4,2,3,1,0:T(8,128)S(1)} %get-tuple-element.103), channel_id=1, source_target_pairs={{2,0},{4,2},{6,4},{8,6},{10,8},{12,10},{14,12},{0,14},{3,1},{5,3},... | collective-permute-start | bytes 122888 | tf_op jit(solution)/shard_map/while/body/eval_jaxpr/ppermute | solution.py:30
  122.5 1.8 %collective-permute-start.3 = (f32[1,2,40,18,1]{2,1,4,3,0:T(2,128)S(1)}, f32[1,2,40,18,1]{2,1,4,3,0:T(2,128)S(1)}, u32[]{:S(2)}, u32[]{:S(2)}) collective-permute-start(f32[1,2,40,18,1]{2,1,4,3,0:T(2,128)S(1)} %copy.34), channel_id=1, source_target_pairs={{1,0},{0,1},{3,2},{2,3},{5,4},{4,5},{7,6},{6,7},{9,8},{8,9},{11,10... | collective-permute-start | bytes 17288 | tf_op jit(solution)/shard_map/while/body/eval_jaxpr/ppermute | solution.py:30
  127.1 6.7 %collective-permute-start = (f32[1,2,40,1,128]{4,2,3,1,0:T(8,128)S(1)}, f32[1,2,40,1,128]{4,2,3,1,0:T(8,128)S(1)}, u32[]{:S(2)}, u32[]{:S(2)}) collective-permute-start(f32[1,2,40,1,128]{4,2,3,1,0:T(8,128)S(1)} %get-tuple-element.102), channel_id=1, source_target_pairs={{0,2},{2,4},{4,6},{6,8},{8,10},{10,12},{12,14},{14,0},{1,3},{3,5},... | collective-permute-start | bytes 122888 | tf_op jit(solution)/shard_map/while/body/eval_jaxpr/ppermute | solution.py:28
  127.1 6.8 %collective-permute-start.1 = (f32[1,2,40,1,128]{4,2,3,1,0:T(8,128)S(1)}, f32[1,2,40,1,128]{4,2,3,1,0:T(8,128)S(1)}, u32[]{:S(2)}, u32[]{:S(2)}) collective-permute-start(f32[1,2,40,1,128]{4,2,3,1,0:T(8,128)S(1)} %get-tuple-element.103), channel_id=1, source_target_pairs={{2,0},{4,2},{6,4},{8,6},{10,8},{12,10},{14,12},{0,14},{3,1},{5,3},... | collective-permute-start | bytes 122888 | tf_op jit(solution)/shard_map/while/body/eval_jaxpr/ppermute | solution.py:30
  134.8 1.8 %collective-permute-start.3 = (f32[1,2,40,18,1]{2,1,4,3,0:T(2,128)S(1)}, f32[1,2,40,18,1]{2,1,4,3,0:T(2,128)S(1)}, u32[]{:S(2)}, u32[]{:S(2)}) collective-permute-start(f32[1,2,40,18,1]{2,1,4,3,0:T(2,128)S(1)} %copy.34), channel_id=1, source_target_pairs={{1,0},{0,1},{3,2},{2,3},{5,4},{4,5},{7,6},{6,7},{9,8},{8,9},{11,10... | collective-permute-start | bytes 17288 | tf_op jit(solution)/shard_map/while/body/eval_jaxpr/ppermute | solution.py:30
  139.4 6.7 %collective-permute-start = (f32[1,2,40,1,128]{4,2,3,1,0:T(8,128)S(1)}, f32[1,2,40,1,128]{4,2,3,1,0:T(8,128)S(1)}, u32[]{:S(2)}, u32[]{:S(2)}) collective-permute-start(f32[1,2,40,1,128]{4,2,3,1,0:T(8,128)S(1)} %get-tuple-element.102), channel_id=1, source_target_pairs={{0,2},{2,4},{4,6},{6,8},{8,10},{10,12},{12,14},{14,0},{1,3},{3,5},... | collective-permute-start | bytes 122888 | tf_op jit(solution)/shard_map/while/body/eval_jaxpr/ppermute | solution.py:28
  139.4 6.7 %collective-permute-start.1 = (f32[1,2,40,1,128]{4,2,3,1,0:T(8,128)S(1)}, f32[1,2,40,1,128]{4,2,3,1,0:T(8,128)S(1)}, u32[]{:S(2)}, u32[]{:S(2)}) collective-permute-start(f32[1,2,40,1,128]{4,2,3,1,0:T(8,128)S(1)} %get-tuple-element.103), channel_id=1, source_target_pairs={{2,0},{4,2},{6,4},{8,6},{10,8},{12,10},{14,12},{0,14},{3,1},{5,3},... | collective-permute-start | bytes 122888 | tf_op jit(solution)/shard_map/while/body/eval_jaxpr/ppermute | solution.py:30
  147.0 1.8 %collective-permute-start.3 = (f32[1,2,40,18,1]{2,1,4,3,0:T(2,128)S(1)}, f32[1,2,40,18,1]{2,1,4,3,0:T(2,128)S(1)}, u32[]{:S(2)}, u32[]{:S(2)}) collective-permute-start(f32[1,2,40,18,1]{2,1,4,3,0:T(2,128)S(1)} %copy.34), channel_id=1, source_target_pairs={{1,0},{0,1},{3,2},{2,3},{5,4},{4,5},{7,6},{6,7},{9,8},{8,9},{11,10... | collective-permute-start | bytes 17288 | tf_op jit(solution)/shard_map/while/body/eval_jaxpr/ppermute | solution.py:30
  151.7 6.7 %collective-permute-start = (f32[1,2,40,1,128]{4,2,3,1,0:T(8,128)S(1)}, f32[1,2,40,1,128]{4,2,3,1,0:T(8,128)S(1)}, u32[]{:S(2)}, u32[]{:S(2)}) collective-permute-start(f32[1,2,40,1,128]{4,2,3,1,0:T(8,128)S(1)} %get-tuple-element.102), channel_id=1, source_target_pairs={{0,2},{2,4},{4,6},{6,8},{8,10},{10,12},{12,14},{14,0},{1,3},{3,5},... | collective-permute-start | bytes 122888 | tf_op jit(solution)/shard_map/while/body/eval_jaxpr/ppermute | solution.py:28
  151.7 6.8 %collective-permute-start.1 = (f32[1,2,40,1,128]{4,2,3,1,0:T(8,128)S(1)}, f32[1,2,40,1,128]{4,2,3,1,0:T(8,128)S(1)}, u32[]{:S(2)}, u32[]{:S(2)}) collective-permute-start(f32[1,2,40,1,128]{4,2,3,1,0:T(8,128)S(1)} %get-tuple-element.103), channel_id=1, source_target_pairs={{2,0},{4,2},{6,4},{8,6},{10,8},{12,10},{14,12},{0,14},{3,1},{5,3},... | collective-permute-start | bytes 122888 | tf_op jit(solution)/shard_map/while/body/eval_jaxpr/ppermute | solution.py:30
  (13 other events, 47.7 us)
Sparse Core Ops, SparseCore 0:
  10.0 26.9 all-gather.1
where the time goes:
time: 172 us
  starting transfers between devices  57.3 us (33%)
  waiting for transfers between devices  49.7 us (29%)
  local copies, waits for them, and re-layouts  29.9 us (17%)
  other arithmetic  17.9 us (10%)
  between operations  13.4 us (8%)
  matrix products  3.01 us (2%)
    ppermute x20, starting transfers between devices, padded(): lax.ppermute(head, axis, [((i + 1) % count, i) for i in range(count)])  45.2 us
    ppermute x20, waiting for transfers between devices, padded(): lax.ppermute(tail, axis, [(i, (i + 1) % count) for i in range(count)])  27.5 us
    all_gather x1, waiting for transfers between devices, per_device(): lax.all_gather(masked, 'lev', axis=2, tiled=True)  19.4 us
    while x50, local copies, waits for them, and re-layouts  17.4 us
    mul x10, other arithmetic, relax(): return wet_center * (center + flux)  14.5 us
    ppermute x20, starting transfers between devices, padded(): lax.ppermute(tail, axis, [(i, (i + 1) % count) for i in range(count)])  7.65 us
  transfers between devices with their start and end apart: 43, of which 23 were waited for; matrix products, arithmetic and copies ran while one was open for 3% of the time, Pallas kernels for 0%

commit v1 on v0

--- a/solution.py
+++ b/solution.py
@@ -4,6 +4,18 @@
 from jax.sharding import PartitionSpec as P
 
 PASSES = 10
+
+
+def gather_by_bits(x, axis, dim):
+    ways, here = (lax.axis_size(axis), lax.axis_index(axis))
+    grown, reach = (x, 1)
+    while reach < ways:
+        theirs = lax.ppermute(grown, axis, [(d, d ^ reach) for d in range(ways)])
+        mine_first = jnp.concatenate([grown, theirs], axis=dim)
+        theirs_first = jnp.concatenate([theirs, grown], axis=dim)
+        grown = jnp.where(here & reach == 0, mine_first, theirs_first)
+        reach = 2 * reach
+    return grown
 
 
 def from_behind(block, axis, distance):
@@ -56,7 +68,7 @@
     correlated = jnp.einsum(
         "toh,dthxy->dtoxy",
         own_rows,
-        lax.all_gather(masked, "lev", axis=2, tiled=True),
+        gather_by_bits(masked, "lev", 2),
         precision=lax.Precision.HIGHEST,
     )
     field = correlated * wet_float

time: 172 us -> 151 us (0.88)
  between operations: 13.4 us -> 0.07 us
  waiting for transfers between devices: 49.7 us -> 41 us
    all_gather x1 -> x0, waiting for transfers between devices: 19.4 us -> none  [per_device(): lax.all_gather(masked, 'lev', axis=2, tiled=True)]
    ppermute x0 -> x1, waiting for transfers between devices: none -> 13.4 us  [gather_by_bits(): theirs = lax.ppermute(grown, axis, [(d, d ^ reach) for d in range(ways)])]
    ppermute x1, waiting for transfers between devices: 2.12 us -> 0.01 us  [from_behind(): return lax.ppermute(block, axis, route)]
    mul x1, other arithmetic: 2.14 us -> 0.21 us  [per_device(): masked = increments * wet_float]
  transfers between devices with their start and end apart: 43 -> 43, of which waited for: 23 -> 21; matrix products, arithmetic and copies ran while one was open for 3% -> 5% of each run, Pallas kernels for 0% -> 0%
where the time goes in v1:
time: 151 us; the launch traced here: 150 us
  starting transfers between devices  58.8 us (39%)
  waiting for transfers between devices  41 us (27%)
  local copies, waits for them, and re-layouts  31.1 us (21%)
  other arithmetic  16.8 us (11%)
  matrix products  1.77 us (1%)
    ppermute x20, starting transfers between devices, padded(): lax.ppermute(head, axis, [((i + 1) % count, i) for i in range(count)])  45.2 us
    ppermute x20, waiting for transfers between devices, padded(): lax.ppermute(tail, axis, [(i, (i + 1) % count) for i in range(count)])  27.5 us
    while x50, local copies, waits for them, and re-layouts  17.4 us
    mul x10, other arithmetic, relax(): return wet_center * (center + flux)  14.4 us
    ppermute x1, waiting for transfers between devices, gather_by_bits(): theirs = lax.ppermute(grown, axis, [(d, d ^ reach) for d in range(ways)])  13.4 us
    ppermute x20, starting transfers between devices, padded(): lax.ppermute(tail, axis, [(i, (i + 1) % count) for i in range(count)])  7.68 us
    ppermute x10, local copies, waits for them, and re-layouts, padded(): lax.ppermute(head, axis, [((i + 1) % count, i) for i in range(count)])  3.31 us
    ppermute x10, local copies, waits for them, and re-layouts, padded(): lax.ppermute(tail, axis, [(i, (i + 1) % count) for i in range(count)])  3.3 us
  transfers between devices with their start and end apart: 43, of which 21 were waited for; matrix products, arithmetic and copies ran while one was open for 5% of the time, Pallas kernels for 0%

profile of v1, /device:TPU:0, one launch (start us, length us, event | category | flops | bytes accessed | tf_op | source)
XLA Modules:
  0.0 150.1 jit_solution(8482062386391403629)
XLA Ops:
  0.8 3.0 %collective-permute-start.5 = (f32[1,128]{1,0:T(1,128)S(1)}, f32[1,128]{1,0:T(1,128)S(1)}, u32[]{:S(2)}, u32[]{:S(2)}) collective-permute-start(f32[1,128]{1,0:T(1,128)S(1)} %slice_bitcast_fusion.1), channel_id=1, source_target_pairs={{14,0},{0,2},{2,4},{4,6},{6,8},{8,10},{10,12},{12,14},{15,1},{1,3}... | collective-permute-start | bytes 1544 | tf_op jit(solution)/shard_map/ppermute | solution.py:24
  4.5 1.4 collective-permute-start.6
  7.3 1.6 %collective-permute-start.4 = (f32[1,2,40,16,128]{4,2,3,1,0:T(8,128)S(1)}, f32[1,2,40,16,128]{4,2,3,1,0:T(8,128)S(1)}, u32[]{:S(2)}, u32[]{:S(2)}) collective-permute-start(f32[1,2,40,16,128]{4,2,3,1,0:T(8,128)S(1)} %copy_multiply_fusion), channel_id=1, source_target_pairs={{0,16},{16,0},{1,17},{17,1},{2,18},{18,2},{3,19},{19,3},{4,20},{20... | collective-permute-start | bytes 1966088 | tf_op jit(solution)/shard_map/ppermute | solution.py:13
  10.0 13.4 %collective-permute-done.4 = f32[1,2,40,16,128]{4,2,3,1,0:T(8,128)S(1)} collective-permute-done((f32[1,2,40,16,128]{4,2,3,1,0:T(8,128)S(1)}, f32[1,2,40,16,128]{4,2,3,1,0:T(8,128)S(1)}, u32[]{:S(2)}, u32[]{:S(2)}) %collective-permute-start.4) | collective-permute-done | bytes 655392 | tf_op jit(solution)/shard_map/ppermute | solution.py:13
  23.4 1.8 %fusion.20 = f32[1,2,40,16,128]{4,2,3,1,0:T(8,128)} fusion(f32[2,40,16,128]{3,1,2,0:T(8,128)S(1)} %bitcast.22, f32[2,40,16,128]{3,1,2,0:T(8,128)S(1)} %fusion.31, pred[]{:T(512)S(6)} %eq.3, f32[40,16,128]{2,0,1:T(8,128)S(1)} %fusion.22, f32[2,80,80]{2,1,0:T(8,128)S(1)} %copy-done, s32[]{:T(128)S(6)} %select_n.16), kind=kOutput, calls=%fused_computation.28 | convolution fusion | flops 158433280 | bytes 2334725 | tf_op jit(solution)/shard_map/toh,dthxy->dtoxy/dot_general | solution.py:68
  25.2 122.9 %while.10 = (s32[]{:T(128)}, f32[1,2,40,16,128]{4,2,3,1,0:T(8,128)}, f32[40,16,128]{2,0,1:T(8,128)S(1)}, f32[18,130]{1,0:T(8,128)S(1)}, f32[18,130]{1,0:T(8,128)S(1)}, /*index=5*/s32[]{:T(128)}) while((s32[]{:T(128)}, f32[1,2,40,16,128]{4,2,3,1,0:T(8,128)}, f32[40,16,128]{2,0,1:T(8,128)S(1)}, f32[18,130]{1,0:T(8,128)S(1)}, ...), condition=%wide.region_1.2_spmd, body=%wide.region_0.1_spmd.sunk | while | flops 2785282 | bytes 5959653 | solution.py:93
  26.3 1.5 %collective-permute-start = (f32[1,2,40,1,128]{4,2,3,1,0:T(8,128)S(1)}, f32[1,2,40,1,128]{4,2,3,1,0:T(8,128)S(1)}, u32[]{:S(2)}, u32[]{:S(2)}) collective-permute-start(f32[1,2,40,1,128]{4,2,3,1,0:T(8,128)S(1)} %get-tuple-element.102), channel_id=1, source_target_pairs={{0,2},{2,4},{4,6},{6,8},{8,10},{10,12},{12,14},{14,0},{1,3},{3,5},... | collective-permute-start | bytes 122888 | tf_op jit(solution)/shard_map/while/body/eval_jaxpr/ppermute | solution.py:40
  27.8 3.2 %collective-permute-start.1 = (f32[1,2,40,1,128]{4,2,3,1,0:T(8,128)S(1)}, f32[1,2,40,1,128]{4,2,3,1,0:T(8,128)S(1)}, u32[]{:S(2)}, u32[]{:S(2)}) collective-permute-start(f32[1,2,40,1,128]{4,2,3,1,0:T(8,128)S(1)} %get-tuple-element.103), channel_id=1, source_target_pairs={{2,0},{4,2},{6,4},{8,6},{10,8},{12,10},{14,12},{0,14},{3,1},{5,3},... | collective-permute-start | bytes 122888 | tf_op jit(solution)/shard_map/while/body/eval_jaxpr/ppermute | solution.py:42
  31.0 2.0 %collective-permute-done = f32[1,2,40,1,128]{4,2,3,1,0:T(8,128)S(1)} collective-permute-done((f32[1,2,40,1,128]{4,2,3,1,0:T(8,128)S(1)}, f32[1,2,40,1,128]{4,2,3,1,0:T(8,128)S(1)}, u32[]{:S(2)}, u32[]{:S(2)}) %collective-permute-start) | collective-permute-done | bytes 40992 | tf_op jit(solution)/shard_map/while/body/eval_jaxpr/ppermute | solution.py:40
  36.0 1.4 fusion.39
  39.7 3.6 %collective-permute-start.1 = (f32[1,2,40,1,128]{4,2,3,1,0:T(8,128)S(1)}, f32[1,2,40,1,128]{4,2,3,1,0:T(8,128)S(1)}, u32[]{:S(2)}, u32[]{:S(2)}) collective-permute-start(f32[1,2,40,1,128]{4,2,3,1,0:T(8,128)S(1)} %get-tuple-element.103), channel_id=1, source_target_pairs={{2,0},{4,2},{6,4},{8,6},{10,8},{12,10},{14,12},{0,14},{3,1},{5,3},... | collective-permute-start | bytes 122888 | tf_op jit(solution)/shard_map/while/body/eval_jaxpr/ppermute | solution.py:42
  43.3 2.0 %collective-permute-done = f32[1,2,40,1,128]{4,2,3,1,0:T(8,128)S(1)} collective-permute-done((f32[1,2,40,1,128]{4,2,3,1,0:T(8,128)S(1)}, f32[1,2,40,1,128]{4,2,3,1,0:T(8,128)S(1)}, u32[]{:S(2)}, u32[]{:S(2)}) %collective-permute-start) | collective-permute-done | bytes 40992 | tf_op jit(solution)/shard_map/while/body/eval_jaxpr/ppermute | solution.py:40
  48.3 1.4 fusion.39
  50.8 4.7 %collective-permute-start.1 = (f32[1,2,40,1,128]{4,2,3,1,0:T(8,128)S(1)}, f32[1,2,40,1,128]{4,2,3,1,0:T(8,128)S(1)}, u32[]{:S(2)}, u32[]{:S(2)}) collective-permute-start(f32[1,2,40,1,128]{4,2,3,1,0:T(8,128)S(1)} %get-tuple-element.103), channel_id=1, source_target_pairs={{2,0},{4,2},{6,4},{8,6},{10,8},{12,10},{14,12},{0,14},{3,1},{5,3},... | collective-permute-start | bytes 122888 | tf_op jit(solution)/shard_map/while/body/eval_jaxpr/ppermute | solution.py:42
  55.6 2.0 %collective-permute-done = f32[1,2,40,1,128]{4,2,3,1,0:T(8,128)S(1)} collective-permute-done((f32[1,2,40,1,128]{4,2,3,1,0:T(8,128)S(1)}, f32[1,2,40,1,128]{4,2,3,1,0:T(8,128)S(1)}, u32[]{:S(2)}, u32[]{:S(2)}) %collective-permute-start) | collective-permute-done | bytes 40992 | tf_op jit(solution)/shard_map/while/body/eval_jaxpr/ppermute | solution.py:40
  63.1 4.7 %collective-permute-start.1 = (f32[1,2,40,1,128]{4,2,3,1,0:T(8,128)S(1)}, f32[1,2,40,1,128]{4,2,3,1,0:T(8,128)S(1)}, u32[]{:S(2)}, u32[]{:S(2)}) collective-permute-start(f32[1,2,40,1,128]{4,2,3,1,0:T(8,128)S(1)} %get-tuple-element.103), channel_id=1, source_target_pairs={{2,0},{4,2},{6,4},{8,6},{10,8},{12,10},{14,12},{0,14},{3,1},{5,3},... | collective-permute-start | bytes 122888 | tf_op jit(solution)/shard_map/while/body/eval_jaxpr/ppermute | solution.py:42
  67.8 2.0 %collective-permute-done = f32[1,2,40,1,128]{4,2,3,1,0:T(8,128)S(1)} collective-permute-done((f32[1,2,40,1,128]{4,2,3,1,0:T(8,128)S(1)}, f32[1,2,40,1,128]{4,2,3,1,0:T(8,128)S(1)}, u32[]{:S(2)}, u32[]{:S(2)}) %collective-permute-start) | collective-permute-done | bytes 40992 | tf_op jit(solution)/shard_map/while/body/eval_jaxpr/ppermute | solution.py:40
  75.4 4.7 %collective-permute-start.1 = (f32[1,2,40,1,128]{4,2,3,1,0:T(8,128)S(1)}, f32[1,2,40,1,128]{4,2,3,1,0:T(8,128)S(1)}, u32[]{:S(2)}, u32[]{:S(2)}) collective-permute-start(f32[1,2,40,1,128]{4,2,3,1,0:T(8,128)S(1)} %get-tuple-element.103), channel_id=1, source_target_pairs={{2,0},{4,2},{6,4},{8,6},{10,8},{12,10},{14,12},{0,14},{3,1},{5,3},... | collective-permute-start | bytes 122888 | tf_op jit(solution)/shard_map/while/body/eval_jaxpr/ppermute | solution.py:42
  80.1 2.0 %collective-permute-done = f32[1,2,40,1,128]{4,2,3,1,0:T(8,128)S(1)} collective-permute-done((f32[1,2,40,1,128]{4,2,3,1,0:T(8,128)S(1)}, f32[1,2,40,1,128]{4,2,3,1,0:T(8,128)S(1)}, u32[]{:S(2)}, u32[]{:S(2)}) %collective-permute-start) | collective-permute-done | bytes 40992 | tf_op jit(solution)/shard_map/while/body/eval_jaxpr/ppermute | solution.py:40
  87.7 4.7 %collective-permute-start.1 = (f32[1,2,40,1,128]{4,2,3,1,0:T(8,128)S(1)}, f32[1,2,40,1,128]{4,2,3,1,0:T(8,128)S(1)}, u32[]{:S(2)}, u32[]{:S(2)}) collective-permute-start(f32[1,2,40,1,128]{4,2,3,1,0:T(8,128)S(1)} %get-tuple-element.103), channel_id=1, source_target_pairs={{2,0},{4,2},{6,4},{8,6},{10,8},{12,10},{14,12},{0,14},{3,1},{5,3},... | collective-permute-start | bytes 122888 | tf_op jit(solution)/shard_map/while/body/eval_jaxpr/ppermute | solution.py:42
  92.4 2.0 %collective-permute-done = f32[1,2,40,1,128]{4,2,3,1,0:T(8,128)S(1)} collective-permute-done((f32[1,2,40,1,128]{4,2,3,1,0:T(8,128)S(1)}, f32[1,2,40,1,128]{4,2,3,1,0:T(8,128)S(1)}, u32[]{:S(2)}, u32[]{:S(2)}) %collective-permute-start) | collective-permute-done | bytes 40992 | tf_op jit(solution)/shard_map/while/body/eval_jaxpr/ppermute | solution.py:40
  100.0 4.7 %collective-permute-start.1 = (f32[1,2,40,1,128]{4,2,3,1,0:T(8,128)S(1)}, f32[1,2,40,1,128]{4,2,3,1,0:T(8,128)S(1)}, u32[]{:S(2)}, u32[]{:S(2)}) collective-permute-start(f32[1,2,40,1,128]{4,2,3,1,0:T(8,128)S(1)} %get-tuple-element.103), channel_id=1, source_target_pairs={{2,0},{4,2},{6,4},{8,6},{10,8},{12,10},{14,12},{0,14},{3,1},{5,3},... | collective-permute-start | bytes 122888 | tf_op jit(solution)/shard_map/while/body/eval_jaxpr/ppermute | solution.py:42
  104.7 2.0 %collective-permute-done = f32[1,2,40,1,128]{4,2,3,1,0:T(8,128)S(1)} collective-permute-done((f32[1,2,40,1,128]{4,2,3,1,0:T(8,128)S(1)}, f32[1,2,40,1,128]{4,2,3,1,0:T(8,128)S(1)}, u32[]{:S(2)}, u32[]{:S(2)}) %collective-permute-start) | collective-permute-done | bytes 40992 | tf_op jit(solution)/shard_map/while/body/eval_jaxpr/ppermute | solution.py:40
  112.3 4.7 %collective-permute-start.1 = (f32[1,2,40,1,128]{4,2,3,1,0:T(8,128)S(1)}, f32[1,2,40,1,128]{4,2,3,1,0:T(8,128)S(1)}, u32[]{:S(2)}, u32[]{:S(2)}) collective-permute-start(f32[1,2,40,1,128]{4,2,3,1,0:T(8,128)S(1)} %get-tuple-element.103), channel_id=1, source_target_pairs={{2,0},{4,2},{6,4},{8,6},{10,8},{12,10},{14,12},{0,14},{3,1},{5,3},... | collective-permute-start | bytes 122888 | tf_op jit(solution)/shard_map/while/body/eval_jaxpr/ppermute | solution.py:42
  117.0 2.0 %collective-permute-done = f32[1,2,40,1,128]{4,2,3,1,0:T(8,128)S(1)} collective-permute-done((f32[1,2,40,1,128]{4,2,3,1,0:T(8,128)S(1)}, f32[1,2,40,1,128]{4,2,3,1,0:T(8,128)S(1)}, u32[]{:S(2)}, u32[]{:S(2)}) %collective-permute-start) | collective-permute-done | bytes 40992 | tf_op jit(solution)/shard_map/while/body/eval_jaxpr/ppermute | solution.py:40
  122.0 1.4 fusion.39
  124.6 4.7 %collective-permute-start.1 = (f32[1,2,40,1,128]{4,2,3,1,0:T(8,128)S(1)}, f32[1,2,40,1,128]{4,2,3,1,0:T(8,128)S(1)}, u32[]{:S(2)}, u32[]{:S(2)}) collective-permute-start(f32[1,2,40,1,128]{4,2,3,1,0:T(8,128)S(1)} %get-tuple-element.103), channel_id=1, source_target_pairs={{2,0},{4,2},{6,4},{8,6},{10,8},{12,10},{14,12},{0,14},{3,1},{5,3},... | collective-permute-start | bytes 122888 | tf_op jit(solution)/shard_map/while/body/eval_jaxpr/ppermute | solution.py:42
  129.3 2.0 %collective-permute-done = f32[1,2,40,1,128]{4,2,3,1,0:T(8,128)S(1)} collective-permute-done((f32[1,2,40,1,128]{4,2,3,1,0:T(8,128)S(1)}, f32[1,2,40,1,128]{4,2,3,1,0:T(8,128)S(1)}, u32[]{:S(2)}, u32[]{:S(2)}) %collective-permute-start) | collective-permute-done | bytes 40992 | tf_op jit(solution)/shard_map/while/body/eval_jaxpr/ppermute | solution.py:40
  136.8 4.7 %collective-permute-start.1 = (f32[1,2,40,1,128]{4,2,3,1,0:T(8,128)S(1)}, f32[1,2,40,1,128]{4,2,3,1,0:T(8,128)S(1)}, u32[]{:S(2)}, u32[]{:S(2)}) collective-permute-start(f32[1,2,40,1,128]{4,2,3,1,0:T(8,128)S(1)} %get-tuple-element.103), channel_id=1, source_target_pairs={{2,0},{4,2},{6,4},{8,6},{10,8},{12,10},{14,12},{0,14},{3,1},{5,3},... | collective-permute-start | bytes 122888 | tf_op jit(solution)/shard_map/while/body/eval_jaxpr/ppermute | solution.py:42
  141.6 2.0 %collective-permute-done = f32[1,2,40,1,128]{4,2,3,1,0:T(8,128)S(1)} collective-permute-done((f32[1,2,40,1,128]{4,2,3,1,0:T(8,128)S(1)}, f32[1,2,40,1,128]{4,2,3,1,0:T(8,128)S(1)}, u32[]{:S(2)}, u32[]{:S(2)}) %collective-permute-start) | collective-permute-done | bytes 40992 | tf_op jit(solution)/shard_map/while/body/eval_jaxpr/ppermute | solution.py:40
  146.6 1.4 fusion.39
  148.0 2.0 %copy.20 = f32[1,2,40,16,128]{4,3,2,1,0:T(8,128)} copy(f32[1,2,40,16,128]{4,2,3,1,0:T(8,128)} %get-tuple-element.32) | data formatting | bytes 1310720 | tf_op jit(solution)/shard_map/while | solution.py:93
  (198 shorter events, 54.7 us)
Async XLA Ops:
  0.8 9.1 %collective-permute-start.5 = (f32[1,128]{1,0:T(1,128)S(1)}, f32[1,128]{1,0:T(1,128)S(1)}, u32[]{:S(2)}, u32[]{:S(2)}) collective-permute-start(f32[1,128]{1,0:T(1,128)S(1)} %slice_bitcast_fusion.1), channel_id=1, source_target_pairs={{14,0},{0,2},{2,4},{4,6},{6,8},{8,10},{10,12},{12,14},{15,1},{1,3}... | collective-permute-start | bytes 1544 | tf_op jit(solution)/shard_map/ppermute | solution.py:24
  4.5 5.2 %collective-permute-start.6 = (f32[16,1]{1,0:T(8,128)S(1)}, f32[16,1]{1,0:T(8,128)S(1)}, u32[]{:S(2)}, u32[]{:S(2)}) collective-permute-start(f32[16,1]{1,0:T(8,128)S(1)} %slice.63), channel_id=1, source_target_pairs={{0,1},{2,3},{4,5},{6,7},{8,9},{10,11},{12,13},{14,15},{16,17},{18,... | collective-permute-start | bytes 200 | tf_op jit(solution)/shard_map/ppermute | solution.py:30
  7.3 16.1 %collective-permute-start.4 = (f32[1,2,40,16,128]{4,2,3,1,0:T(8,128)S(1)}, f32[1,2,40,16,128]{4,2,3,1,0:T(8,128)S(1)}, u32[]{:S(2)}, u32[]{:S(2)}) collective-permute-start(f32[1,2,40,16,128]{4,2,3,1,0:T(8,128)S(1)} %copy_multiply_fusion), channel_id=1, source_target_pairs={{0,16},{16,0},{1,17},{17,1},{2,18},{18,2},{3,19},{19,3},{4,20},{20... | collective-permute-start | bytes 1966088 | tf_op jit(solution)/shard_map/ppermute | solution.py:13
  26.3 6.7 %collective-permute-start = (f32[1,2,40,1,128]{4,2,3,1,0:T(8,128)S(1)}, f32[1,2,40,1,128]{4,2,3,1,0:T(8,128)S(1)}, u32[]{:S(2)}, u32[]{:S(2)}) collective-permute-start(f32[1,2,40,1,128]{4,2,3,1,0:T(8,128)S(1)} %get-tuple-element.102), channel_id=1, source_target_pairs={{0,2},{2,4},{4,6},{6,8},{8,10},{10,12},{12,14},{14,0},{1,3},{3,5},... | collective-permute-start | bytes 122888 | tf_op jit(solution)/shard_map/while/body/eval_jaxpr/ppermute | solution.py:40
  27.8 5.2 %collective-permute-start.1 = (f32[1,2,40,1,128]{4,2,3,1,0:T(8,128)S(1)}, f32[1,2,40,1,128]{4,2,3,1,0:T(8,128)S(1)}, u32[]{:S(2)}, u32[]{:S(2)}) collective-permute-start(f32[1,2,40,1,128]{4,2,3,1,0:T(8,128)S(1)} %get-tuple-element.103), channel_id=1, source_target_pairs={{2,0},{4,2},{6,4},{8,6},{10,8},{12,10},{14,12},{0,14},{3,1},{5,3},... | collective-permute-start | bytes 122888 | tf_op jit(solution)/shard_map/while/body/eval_jaxpr/ppermute | solution.py:42
  33.9 1.8 %collective-permute-start.3 = (f32[1,2,40,18,1]{2,1,4,3,0:T(2,128)S(1)}, f32[1,2,40,18,1]{2,1,4,3,0:T(2,128)S(1)}, u32[]{:S(2)}, u32[]{:S(2)}) collective-permute-start(f32[1,2,40,18,1]{2,1,4,3,0:T(2,128)S(1)} %copy.36), channel_id=1, source_target_pairs={{1,0},{0,1},{3,2},{2,3},{5,4},{4,5},{7,6},{6,7},{9,8},{8,9},{11,10... | collective-permute-start | bytes 17288 | tf_op jit(solution)/shard_map/while/body/eval_jaxpr/ppermute | solution.py:42
  38.5 6.7 %collective-permute-start = (f32[1,2,40,1,128]{4,2,3,1,0:T(8,128)S(1)}, f32[1,2,40,1,128]{4,2,3,1,0:T(8,128)S(1)}, u32[]{:S(2)}, u32[]{:S(2)}) collective-permute-start(f32[1,2,40,1,128]{4,2,3,1,0:T(8,128)S(1)} %get-tuple-element.102), channel_id=1, source_target_pairs={{0,2},{2,4},{4,6},{6,8},{8,10},{10,12},{12,14},{14,0},{1,3},{3,5},... | collective-permute-start | bytes 122888 | tf_op jit(solution)/shard_map/while/body/eval_jaxpr/ppermute | solution.py:40
  39.7 5.6 %collective-permute-start.1 = (f32[1,2,40,1,128]{4,2,3,1,0:T(8,128)S(1)}, f32[1,2,40,1,128]{4,2,3,1,0:T(8,128)S(1)}, u32[]{:S(2)}, u32[]{:S(2)}) collective-permute-start(f32[1,2,40,1,128]{4,2,3,1,0:T(8,128)S(1)} %get-tuple-element.103), channel_id=1, source_target_pairs={{2,0},{4,2},{6,4},{8,6},{10,8},{12,10},{14,12},{0,14},{3,1},{5,3},... | collective-permute-start | bytes 122888 | tf_op jit(solution)/shard_map/while/body/eval_jaxpr/ppermute | solution.py:42
  46.2 1.8 %collective-permute-start.3 = (f32[1,2,40,18,1]{2,1,4,3,0:T(2,128)S(1)}, f32[1,2,40,18,1]{2,1,4,3,0:T(2,128)S(1)}, u32[]{:S(2)}, u32[]{:S(2)}) collective-permute-start(f32[1,2,40,18,1]{2,1,4,3,0:T(2,128)S(1)} %copy.36), channel_id=1, source_target_pairs={{1,0},{0,1},{3,2},{2,3},{5,4},{4,5},{7,6},{6,7},{9,8},{8,9},{11,10... | collective-permute-start | bytes 17288 | tf_op jit(solution)/shard_map/while/body/eval_jaxpr/ppermute | solution.py:42
  50.8 6.7 %collective-permute-start = (f32[1,2,40,1,128]{4,2,3,1,0:T(8,128)S(1)}, f32[1,2,40,1,128]{4,2,3,1,0:T(8,128)S(1)}, u32[]{:S(2)}, u32[]{:S(2)}) collective-permute-start(f32[1,2,40,1,128]{4,2,3,1,0:T(8,128)S(1)} %get-tuple-element.102), channel_id=1, source_target_pairs={{0,2},{2,4},{4,6},{6,8},{8,10},{10,12},{12,14},{14,0},{1,3},{3,5},... | collective-permute-start | bytes 122888 | tf_op jit(solution)/shard_map/while/body/eval_jaxpr/ppermute | solution.py:40
  50.8 6.7 %collective-permute-start.1 = (f32[1,2,40,1,128]{4,2,3,1,0:T(8,128)S(1)}, f32[1,2,40,1,128]{4,2,3,1,0:T(8,128)S(1)}, u32[]{:S(2)}, u32[]{:S(2)}) collective-permute-start(f32[1,2,40,1,128]{4,2,3,1,0:T(8,128)S(1)} %get-tuple-element.103), channel_id=1, source_target_pairs={{2,0},{4,2},{6,4},{8,6},{10,8},{12,10},{14,12},{0,14},{3,1},{5,3},... | collective-permute-start | bytes 122888 | tf_op jit(solution)/shard_map/while/body/eval_jaxpr/ppermute | solution.py:42
  58.5 1.8 %collective-permute-start.3 = (f32[1,2,40,18,1]{2,1,4,3,0:T(2,128)S(1)}, f32[1,2,40,18,1]{2,1,4,3,0:T(2,128)S(1)}, u32[]{:S(2)}, u32[]{:S(2)}) collective-permute-start(f32[1,2,40,18,1]{2,1,4,3,0:T(2,128)S(1)} %copy.36), channel_id=1, source_target_pairs={{1,0},{0,1},{3,2},{2,3},{5,4},{4,5},{7,6},{6,7},{9,8},{8,9},{11,10... | collective-permute-start | bytes 17288 | tf_op jit(solution)/shard_map/while/body/eval_jaxpr/ppermute | solution.py:42
  63.1 6.7 %collective-permute-start = (f32[1,2,40,1,128]{4,2,3,1,0:T(8,128)S(1)}, f32[1,2,40,1,128]{4,2,3,1,0:T(8,128)S(1)}, u32[]{:S(2)}, u32[]{:S(2)}) collective-permute-start(f32[1,2,40,1,128]{4,2,3,1,0:T(8,128)S(1)} %get-tuple-element.102), channel_id=1, source_target_pairs={{0,2},{2,4},{4,6},{6,8},{8,10},{10,12},{12,14},{14,0},{1,3},{3,5},... | collective-permute-start | bytes 122888 | tf_op jit(solution)/shard_map/while/body/eval_jaxpr/ppermute | solution.py:40
  63.1 6.8 %collective-permute-start.1 = (f32[1,2,40,1,128]{4,2,3,1,0:T(8,128)S(1)}, f32[1,2,40,1,128]{4,2,3,1,0:T(8,128)S(1)}, u32[]{:S(2)}, u32[]{:S(2)}) collective-permute-start(f32[1,2,40,1,128]{4,2,3,1,0:T(8,128)S(1)} %get-tuple-element.103), channel_id=1, source_target_pairs={{2,0},{4,2},{6,4},{8,6},{10,8},{12,10},{14,12},{0,14},{3,1},{5,3},... | collective-permute-start | bytes 122888 | tf_op jit(solution)/shard_map/while/body/eval_jaxpr/ppermute | solution.py:42
  70.8 1.8 %collective-permute-start.3 = (f32[1,2,40,18,1]{2,1,4,3,0:T(2,128)S(1)}, f32[1,2,40,18,1]{2,1,4,3,0:T(2,128)S(1)}, u32[]{:S(2)}, u32[]{:S(2)}) collective-permute-start(f32[1,2,40,18,1]{2,1,4,3,0:T(2,128)S(1)} %copy.36), channel_id=1, source_target_pairs={{1,0},{0,1},{3,2},{2,3},{5,4},{4,5},{7,6},{6,7},{9,8},{8,9},{11,10... | collective-permute-start | bytes 17288 | tf_op jit(solution)/shard_map/while/body/eval_jaxpr/ppermute | solution.py:42
  75.4 6.7 %collective-permute-start = (f32[1,2,40,1,128]{4,2,3,1,0:T(8,128)S(1)}, f32[1,2,40,1,128]{4,2,3,1,0:T(8,128)S(1)}, u32[]{:S(2)}, u32[]{:S(2)}) collective-permute-start(f32[1,2,40,1,128]{4,2,3,1,0:T(8,128)S(1)} %get-tuple-element.102), channel_id=1, source_target_pairs={{0,2},{2,4},{4,6},{6,8},{8,10},{10,12},{12,14},{14,0},{1,3},{3,5},... | collective-permute-start | bytes 122888 | tf_op jit(solution)/shard_map/while/body/eval_jaxpr/ppermute | solution.py:40
  75.4 6.7 %collective-permute-start.1 = (f32[1,2,40,1,128]{4,2,3,1,0:T(8,128)S(1)}, f32[1,2,40,1,128]{4,2,3,1,0:T(8,128)S(1)}, u32[]{:S(2)}, u32[]{:S(2)}) collective-permute-start(f32[1,2,40,1,128]{4,2,3,1,0:T(8,128)S(1)} %get-tuple-element.103), channel_id=1, source_target_pairs={{2,0},{4,2},{6,4},{8,6},{10,8},{12,10},{14,12},{0,14},{3,1},{5,3},... | collective-permute-start | bytes 122888 | tf_op jit(solution)/shard_map/while/body/eval_jaxpr/ppermute | solution.py:42
  83.1 1.8 %collective-permute-start.3 = (f32[1,2,40,18,1]{2,1,4,3,0:T(2,128)S(1)}, f32[1,2,40,18,1]{2,1,4,3,0:T(2,128)S(1)}, u32[]{:S(2)}, u32[]{:S(2)}) collective-permute-start(f32[1,2,40,18,1]{2,1,4,3,0:T(2,128)S(1)} %copy.36), channel_id=1, source_target_pairs={{1,0},{0,1},{3,2},{2,3},{5,4},{4,5},{7,6},{6,7},{9,8},{8,9},{11,10... | collective-permute-start | bytes 17288 | tf_op jit(solution)/shard_map/while/body/eval_jaxpr/ppermute | solution.py:42
  87.7 6.7 %collective-permute-start = (f32[1,2,40,1,128]{4,2,3,1,0:T(8,128)S(1)}, f32[1,2,40,1,128]{4,2,3,1,0:T(8,128)S(1)}, u32[]{:S(2)}, u32[]{:S(2)}) collective-permute-start(f32[1,2,40,1,128]{4,2,3,1,0:T(8,128)S(1)} %get-tuple-element.102), channel_id=1, source_target_pairs={{0,2},{2,4},{4,6},{6,8},{8,10},{10,12},{12,14},{14,0},{1,3},{3,5},... | collective-permute-start | bytes 122888 | tf_op jit(solution)/shard_map/while/body/eval_jaxpr/ppermute | solution.py:40
  87.7 6.8 %collective-permute-start.1 = (f32[1,2,40,1,128]{4,2,3,1,0:T(8,128)S(1)}, f32[1,2,40,1,128]{4,2,3,1,0:T(8,128)S(1)}, u32[]{:S(2)}, u32[]{:S(2)}) collective-permute-start(f32[1,2,40,1,128]{4,2,3,1,0:T(8,128)S(1)} %get-tuple-element.103), channel_id=1, source_target_pairs={{2,0},{4,2},{6,4},{8,6},{10,8},{12,10},{14,12},{0,14},{3,1},{5,3},... | collective-permute-start | bytes 122888 | tf_op jit(solution)/shard_map/while/body/eval_jaxpr/ppermute | solution.py:42
  95.4 1.8 %collective-permute-start.3 = (f32[1,2,40,18,1]{2,1,4,3,0:T(2,128)S(1)}, f32[1,2,40,18,1]{2,1,4,3,0:T(2,128)S(1)}, u32[]{:S(2)}, u32[]{:S(2)}) collective-permute-start(f32[1,2,40,18,1]{2,1,4,3,0:T(2,128)S(1)} %copy.36), channel_id=1, source_target_pairs={{1,0},{0,1},{3,2},{2,3},{5,4},{4,5},{7,6},{6,7},{9,8},{8,9},{11,10... | collective-permute-start | bytes 17288 | tf_op jit(solution)/shard_map/while/body/eval_jaxpr/ppermute | solution.py:42
  100.0 6.7 %collective-permute-start = (f32[1,2,40,1,128]{4,2,3,1,0:T(8,128)S(1)}, f32[1,2,40,1,128]{4,2,3,1,0:T(8,128)S(1)}, u32[]{:S(2)}, u32[]{:S(2)}) collective-permute-start(f32[1,2,40,1,128]{4,2,3,1,0:T(8,128)S(1)} %get-tuple-element.102), channel_id=1, source_target_pairs={{0,2},{2,4},{4,6},{6,8},{8,10},{10,12},{12,14},{14,0},{1,3},{3,5},... | collective-permute-start | bytes 122888 | tf_op jit(solution)/shard_map/while/body/eval_jaxpr/ppermute | solution.py:40
  100.0 6.7 %collective-permute-start.1 = (f32[1,2,40,1,128]{4,2,3,1,0:T(8,128)S(1)}, f32[1,2,40,1,128]{4,2,3,1,0:T(8,128)S(1)}, u32[]{:S(2)}, u32[]{:S(2)}) collective-permute-start(f32[1,2,40,1,128]{4,2,3,1,0:T(8,128)S(1)} %get-tuple-element.103), channel_id=1, source_target_pairs={{2,0},{4,2},{6,4},{8,6},{10,8},{12,10},{14,12},{0,14},{3,1},{5,3},... | collective-permute-start | bytes 122888 | tf_op jit(solution)/shard_map/while/body/eval_jaxpr/ppermute | solution.py:42
  107.6 1.8 %collective-permute-start.3 = (f32[1,2,40,18,1]{2,1,4,3,0:T(2,128)S(1)}, f32[1,2,40,18,1]{2,1,4,3,0:T(2,128)S(1)}, u32[]{:S(2)}, u32[]{:S(2)}) collective-permute-start(f32[1,2,40,18,1]{2,1,4,3,0:T(2,128)S(1)} %copy.36), channel_id=1, source_target_pairs={{1,0},{0,1},{3,2},{2,3},{5,4},{4,5},{7,6},{6,7},{9,8},{8,9},{11,10... | collective-permute-start | bytes 17288 | tf_op jit(solution)/shard_map/while/body/eval_jaxpr/ppermute | solution.py:42
  112.3 6.7 %collective-permute-start = (f32[1,2,40,1,128]{4,2,3,1,0:T(8,128)S(1)}, f32[1,2,40,1,128]{4,2,3,1,0:T(8,128)S(1)}, u32[]{:S(2)}, u32[]{:S(2)}) collective-permute-start(f32[1,2,40,1,128]{4,2,3,1,0:T(8,128)S(1)} %get-tuple-element.102), channel_id=1, source_target_pairs={{0,2},{2,4},{4,6},{6,8},{8,10},{10,12},{12,14},{14,0},{1,3},{3,5},... | collective-permute-start | bytes 122888 | tf_op jit(solution)/shard_map/while/body/eval_jaxpr/ppermute | solution.py:40
  112.3 6.8 %collective-permute-start.1 = (f32[1,2,40,1,128]{4,2,3,1,0:T(8,128)S(1)}, f32[1,2,40,1,128]{4,2,3,1,0:T(8,128)S(1)}, u32[]{:S(2)}, u32[]{:S(2)}) collective-permute-start(f32[1,2,40,1,128]{4,2,3,1,0:T(8,128)S(1)} %get-tuple-element.103), channel_id=1, source_target_pairs={{2,0},{4,2},{6,4},{8,6},{10,8},{12,10},{14,12},{0,14},{3,1},{5,3},... | collective-permute-start | bytes 122888 | tf_op jit(solution)/shard_map/while/body/eval_jaxpr/ppermute | solution.py:42
  119.9 1.8 %collective-permute-start.3 = (f32[1,2,40,18,1]{2,1,4,3,0:T(2,128)S(1)}, f32[1,2,40,18,1]{2,1,4,3,0:T(2,128)S(1)}, u32[]{:S(2)}, u32[]{:S(2)}) collective-permute-start(f32[1,2,40,18,1]{2,1,4,3,0:T(2,128)S(1)} %copy.36), channel_id=1, source_target_pairs={{1,0},{0,1},{3,2},{2,3},{5,4},{4,5},{7,6},{6,7},{9,8},{8,9},{11,10... | collective-permute-start | bytes 17288 | tf_op jit(solution)/shard_map/while/body/eval_jaxpr/ppermute | solution.py:42
  124.6 6.7 %collective-permute-start = (f32[1,2,40,1,128]{4,2,3,1,0:T(8,128)S(1)}, f32[1,2,40,1,128]{4,2,3,1,0:T(8,128)S(1)}, u32[]{:S(2)}, u32[]{:S(2)}) collective-permute-start(f32[1,2,40,1,128]{4,2,3,1,0:T(8,128)S(1)} %get-tuple-element.102), channel_id=1, source_target_pairs={{0,2},{2,4},{4,6},{6,8},{8,10},{10,12},{12,14},{14,0},{1,3},{3,5},... | collective-permute-start | bytes 122888 | tf_op jit(solution)/shard_map/while/body/eval_jaxpr/ppermute | solution.py:40
  124.6 6.7 %collective-permute-start.1 = (f32[1,2,40,1,128]{4,2,3,1,0:T(8,128)S(1)}, f32[1,2,40,1,128]{4,2,3,1,0:T(8,128)S(1)}, u32[]{:S(2)}, u32[]{:S(2)}) collective-permute-start(f32[1,2,40,1,128]{4,2,3,1,0:T(8,128)S(1)} %get-tuple-element.103), channel_id=1, source_target_pairs={{2,0},{4,2},{6,4},{8,6},{10,8},{12,10},{14,12},{0,14},{3,1},{5,3},... | collective-permute-start | bytes 122888 | tf_op jit(solution)/shard_map/while/body/eval_jaxpr/ppermute | solution.py:42
  136.8 6.7 %collective-permute-start = (f32[1,2,40,1,128]{4,2,3,1,0:T(8,128)S(1)}, f32[1,2,40,1,128]{4,2,3,1,0:T(8,128)S(1)}, u32[]{:S(2)}, u32[]{:S(2)}) collective-permute-start(f32[1,2,40,1,128]{4,2,3,1,0:T(8,128)S(1)} %get-tuple-element.102), channel_id=1, source_target_pairs={{0,2},{2,4},{4,6},{6,8},{8,10},{10,12},{12,14},{14,0},{1,3},{3,5},... | collective-permute-start | bytes 122888 | tf_op jit(solution)/shard_map/while/body/eval_jaxpr/ppermute | solution.py:40
  136.8 6.8 %collective-permute-start.1 = (f32[1,2,40,1,128]{4,2,3,1,0:T(8,128)S(1)}, f32[1,2,40,1,128]{4,2,3,1,0:T(8,128)S(1)}, u32[]{:S(2)}, u32[]{:S(2)}) collective-permute-start(f32[1,2,40,1,128]{4,2,3,1,0:T(8,128)S(1)} %get-tuple-element.103), channel_id=1, source_target_pairs={{2,0},{4,2},{6,4},{8,6},{10,8},{12,10},{14,12},{0,14},{3,1},{5,3},... | collective-permute-start | bytes 122888 | tf_op jit(solution)/shard_map/while/body/eval_jaxpr/ppermute | solution.py:42
  144.5 1.8 %collective-permute-start.3 = (f32[1,2,40,18,1]{2,1,4,3,0:T(2,128)S(1)}, f32[1,2,40,18,1]{2,1,4,3,0:T(2,128)S(1)}, u32[]{:S(2)}, u32[]{:S(2)}) collective-permute-start(f32[1,2,40,18,1]{2,1,4,3,0:T(2,128)S(1)} %copy.36), channel_id=1, source_target_pairs={{1,0},{0,1},{3,2},{2,3},{5,4},{4,5},{7,6},{6,7},{9,8},{8,9},{11,10... | collective-permute-start | bytes 17288 | tf_op jit(solution)/shard_map/while/body/eval_jaxpr/ppermute | solution.py:42
  (14 other events, 46.3 us)
